TPU v7x, 32 devices: a whole 2x2x4 slice. The times are simulated.
32 devices in a mesh: groups: 2 (over y), dp: 4 (over z), tensor: 4 (over x, core).
Axes of the slice: x: 2, y: 2, z: 4, core: 2. Of those that a mesh axis runs over, the one named last changes fastest.
Arguments:
- train_rows: bfloat16 [2048, 5120], P(('groups', 'dp')), parts along dimension 0, may hold values from -40 to 40
- out_grads: bfloat16 [2048, 27648], P(('groups', 'dp'), 'tensor'), parts along dimension 0, may hold values from -6 to 6
- input_factor: bfloat16 [512, 5120], P(('groups', 'dp'), 'tensor'), parts along dimension 0, may hold values from -0.078125 to 0.078125
- output_factor: bfloat16 [512, 27648], P(('groups', 'dp'), 'tensor'), parts along dimension 0, may hold values from -0.0068359375 to 0.0068359375
- train_ids: int32 [2048], P(('groups', 'dp')), parts along dimension 0, may hold values from 0 to 100351
- query_ids: int32 [16], P('groups'), parts along dimension 0, may hold values from 0 to 100351
- loss_weights: float32 [100352], replicated, may hold values from 0.3 to 3
Outputs:
- scores: float32 [8, 2048], P(None, ('groups', 'dp', 'tensor')), parts along dimension 1
There are 2 independent parts, one for each index of `groups`. A program takes and returns all parts, laid end to end along the dimension named above; an argument that names none is the same for every part. Nothing has to cross between parts.
All inputs are finite; a program needn't handle non-finite values.
Results may differ from a plain program's by a relative error of at most 0.0003.
Values may be sent and summed in bfloat16 or wider, within the bound.
A program may use at most 128 MiB of HBM per device.

v0:
```python
import jax
import jax.numpy as jnp
from jax import lax
from jax.sharding import PartitionSpec as P


def contract(operand_left, operand_right):
    return lax.dot_general(
        operand_left, operand_right, (((1,), (1,)), ((), ())), preferred_element_type=jnp.float32
    )


def shards(train_rows, out_grads, input_factor, output_factor, train_ids, query_ids, loss_weights):
    tensor_ways = lax.axis_size("tensor")
    tensor_place = lax.axis_index("tensor")
    tokens_here = train_rows.shape[0]
    row_share = tokens_here // tensor_ways
    width_here = input_factor.shape[1]
    rank_rows = input_factor.shape[0] * lax.axis_size("dp")
    queries = query_ids.shape[0]
    rank_count = rank_rows // queries
    first_row = tensor_place * row_share
    local_inputs = lax.dynamic_slice_in_dim(train_rows, tensor_place * width_here, width_here, 1)
    input_part = contract(local_inputs, lax.all_gather(input_factor, "dp", axis=0, tiled=True))
    grad_part = contract(out_grads, lax.all_gather(output_factor, "dp", axis=0, tiled=True))
    input_whole, grad_whole = lax.psum((input_part, grad_part), "tensor")
    input_proj = lax.dynamic_slice_in_dim(input_whole, first_row, row_share, 0)
    grad_proj = lax.dynamic_slice_in_dim(grad_whole, first_row, row_share, 0)
    raw_scores = (input_proj * grad_proj).reshape(row_share, queries, rank_count).sum(axis=2)
    own_ids = lax.dynamic_slice_in_dim(train_ids, first_row, row_share, 0)
    tok_weight = loss_weights[own_ids]
    query_weight = loss_weights[query_ids]
    return (raw_scores * tok_weight[:, None] * query_weight[None, :]).T


def solution(mesh):
    return jax.shard_map(
        shards,
        mesh=mesh,
        in_specs=(
            P(("groups", "dp"), None),
            P(("groups", "dp"), "tensor"),
            P(("groups", "dp"), "tensor"),
            P(("groups", "dp"), "tensor"),
            P(("groups", "dp")),
            P("groups"),
            P(),
        ),
        out_specs=P(None, ("groups", "dp", "tensor")),
        check_vma=False,
    )
```

profile of v0, /device:TPU:0, one launch (start us, length us, event | category | flops | bytes accessed | tf_op | source)
XLA Modules:
  0.0 132.4 jit_solution(16672378060618273757)
XLA Ops:
  6.5 0.0 copy-start
  6.5 0.0 all-gather.2.cloned.1.call-start
  6.5 0.7 all-gather.2.cloned.1.call-update
  7.3 0.0 all-reduce.3.cloned.1.call-start
  7.3 0.9 compare_select_fusion
  8.3 22.8 %all_gather.6 = bf16[256,1280]{1,0:T(8,128)(2,1)S(1)} all-gather(bf16[64,1280]{1,0:T(8,128)(2,1)} %param.9), channel_id=1, replica_groups=mesh['groups'=2,'dp'=4,'tensor'=4] {'dp'}, dimensions={0}, use_global_device_ids=true | all-gather | bytes 819200 | tf_op jit(solution)/shard_map/all_gather | solution.py:24
  31.1 2.2 %fusion = f32[256,256]{1,0:T(8,128)} fusion(bf16[256,1280]{1,0:T(8,128)(2,1)S(1)} %all_gather.6, bf16[256,5120]{1,0:T(8,128)(2,1)} %param.7, s32[]{:T(128)S(6)} %select_n.14), kind=kOutput, calls=%fused_computation.2 | convolution fusion | flops 167772160 | bytes 1572868 | tf_op jit(solution)/shard_map/dot_general | solution.py:8
  33.3 0.0 copy-start.1
  33.3 50.9 %all-gather.2.cloned.1.call-done = bf16[256,6912]{1,0:T(8,128)(2,1)} async-done(((bf16[64,6912]{1,0:T(8,128)(2,1)}), bf16[256,6912]{1,0:T(8,128)(2,1)}) %all-gather.2.cloned.1.call-update) | async-done | bytes 3538960 | tf_op jit(solution)/shard_map/all_gather | solution.py:25
  84.1 0.0 copy-done
  84.1 3.8 %fusion.3 = f32[256,256]{1,0:T(8,128)} fusion(bf16[256,6912]{1,0:T(8,128)(2,1)S(1)} %copy-done, bf16[256,6912]{1,0:T(8,128)(2,1)} %all-gather.2.cloned.1.call-done), kind=kOutput, calls=%fused_computation.12 | convolution fusion | flops 905969664 | bytes 7340032 | tf_op jit(solution)/shard_map/dot_general | solution.py:8
  87.9 0.0 all-reduce.3.cloned.1.call-update
  88.0 1.6 %gather_fusion.1 = f32[8]{0:T(128)S(1)} fusion(f32[100352]{0:T(1024)} %param.13, s32[1024]{0:T(1024)S(1)} %pad_clamp_fusion), kind=kCustom, calls=%fused_computation.1 | custom fusion | bytes 96 | tf_op jit(solution)/shard_map/gather | solution.py:32
  89.6 0.0 copy-done.1
  89.6 0.1 compare_select_fusion.1
  89.7 1.8 %gather_fusion = f32[64]{0:T(128)S(1)} fusion(f32[100352]{0:T(1024)} %param.13, s32[1024]{0:T(1024)S(1)} %pad_clamp_fusion.1), kind=kCustom, calls=%fused_computation | custom fusion | bytes 768 | tf_op jit(solution)/shard_map/gather | solution.py:31
  91.5 29.4 %all-reduce.3.cloned.1.call-done = (f32[256,256]{1,0:T(8,128)}, f32[256,256]{1,0:T(8,128)}) async-done(((f32[256,256]{1,0:T(8,128)}, f32[256,256]{1,0:T(8,128)}), (f32[256,256]{1,0:T(8,128)}, f32[256,256]{1,0:T(8,128)})) %all-reduce.3.cloned.1.call-update) | async-done | bytes 524304 | tf_op jit(solution)/shard_map/psum | solution.py:26
  120.9 1.5 %dynamic-slice_multiply_fusion = f32[64,256]{1,0:T(8,128)} fusion(f32[256,256]{1,0:T(8,128)} %get-tuple-element.5, s32[]{:T(128)S(6)} %select_n.15, f32[256,256]{1,0:T(8,128)} %get-tuple-element.6), kind=kLoop, calls=%fused_computation.5 | loop fusion | flops 16384 | bytes 196612 | tf_op jit(solution)/shard_map/mul | solution.py:29
  122.4 1.6 %copy.8 = f32[64,256]{0,1:T(8,128)} copy(f32[64,256]{1,0:T(8,128)} %dynamic-slice_multiply_fusion) | data formatting | bytes 131072 | tf_op jit(solution)/shard_map/mul | solution.py:29
  124.0 0.9 bitcast_reduce_fusion
  124.9 0.7 multiply_bitcast_fusion
  (2 shorter events, 0.0 us)
Async XLA Ops:
  6.5 77.6 %copy-start = (bf16[256,6912]{1,0:T(8,128)(2,1)S(1)}, bf16[256,6912]{1,0:T(8,128)(2,1)}, u32[]{:S(2)}) copy-start(bf16[256,6912]{1,0:T(8,128)(2,1)} %param.8) | copy-start | bytes 10616836
  6.5 77.6 %all-gather.2.cloned.1.call-start = ((), (), s32[]{:S(2)}) async-start(), calls=%async_computation | async-start | bytes 4423680 | tf_op jit(solution)/shard_map/all_gather | solution.py:25
  7.3 113.6 %all-reduce.3.cloned.1.call-start = ((), (), s32[]{:S(2)}) async-start(), calls=%async_computation.1 | async-start | bytes 1048576 | tf_op jit(solution)/shard_map/psum | solution.py:26
  33.3 56.4 %copy-start.1 = (s32[256]{0:T(256)S(1)}, s32[256]{0:T(256)}, u32[]{:S(2)}) copy-start(s32[256]{0:T(256)} %param.11) | copy-start | bytes 3076
Sparse Core Ops, SparseCore 0:
  8.9 75.1 all-gather.1
  88.1 32.7 all-reduce.2
where the time goes:
time: 133 us; the launch traced here: 132 us
  waiting for transfers between devices  81 us (61%)
  blocking collectives  22.8 us (17%)
  between operations  13.4 us (10%)
  matrix products  5.99 us (5%)
  local copies, waits for them, and re-layouts  5.01 us (4%)
  other arithmetic  4.14 us (3%)
    all_gather x1, waiting for transfers between devices, shards(): lax.all_gather(output_factor, 'dp', axis=0, tiled=True)  50.9 us
    psum x1, waiting for transfers between devices, shards(): input_whole, grad_whole = lax.psum((input_part, grad_part), 'tensor')  29.4 us
    all_gather x1, blocking collectives, shards(): lax.all_gather(input_factor, 'dp', axis=0, tiled=True)  22.8 us
    dot_general x2, matrix products, contract(): lax.dot_general(operand_left, operand_right, (((1,), (1,)), ((), ())), pr...  5.99 us
  transfers between devices with their start and end apart: 2, of which 2 were waited for; matrix products, arithmetic and copies ran while one was open for 5% of the time, Pallas kernels for 0%

commit v1 on v0

v1 whole, which is shorter than its diff:
```python
import functools

import jax
import jax.numpy as jnp
from jax import lax
from jax.experimental import pallas as pl
from jax.experimental.pallas import tpu as pltpu
from jax.sharding import PartitionSpec as P

LANES = 128
CHUNK_ROWS = 16
K_TILE = 768


def contract(left, right):
    return lax.dot_general(left, right, (((1,), (1,)), ((), ())), preferred_element_type=jnp.float32)


def kernel(
    n, ways, rank_count,
    rows_ref, grads_ref, in_ref, out_factor_ref, table_ref, ids_ref, query_ids_ref,
    scores_ref,
    x_buf, g_buf, in_buf, of_buf, table_buf, proj, landed, tok_buf, query_buf,
    local_sem, in_send, in_recv, of_send, of_recv, sum_send, sum_recv,
):
    place = lax.axis_index("dp")
    tensor_place = lax.axis_index("tensor")
    factor_rows, width = in_ref.shape
    hidden = out_factor_ref.shape[1]
    queries = query_ids_ref.shape[0]
    share = scores_ref.shape[1]
    chunks = factor_rows // CHUNK_ROWS
    has_left = place > 0
    has_right = place < n - 1

    local = [
        pltpu.make_async_copy(grads_ref, g_buf, local_sem.at[0]),
        pltpu.make_async_copy(
            rows_ref.at[:, pl.ds(pl.multiple_of(tensor_place * width, LANES), width)], x_buf, local_sem.at[1]
        ),
        pltpu.make_async_copy(out_factor_ref, of_buf.at[place], local_sem.at[2]),
        pltpu.make_async_copy(in_ref, in_buf.at[place], local_sem.at[3]),
        pltpu.make_async_copy(table_ref, table_buf, local_sem.at[4]),
    ]

    barrier = pltpu.get_barrier_semaphore()

    @pl.when(has_left)
    def _():
        pl.semaphore_signal(barrier, inc=1, device_id={"dp": place - 1}, device_id_type=pl.DeviceIdType.MESH)

    @pl.when(has_right)
    def _():
        pl.semaphore_signal(barrier, inc=1, device_id={"dp": place + 1}, device_id_type=pl.DeviceIdType.MESH)

    for step in range(1, ways):
        pl.semaphore_signal(
            barrier, inc=1, device_id={"tensor": lax.rem(tensor_place + step, ways)},
            device_id_type=pl.DeviceIdType.MESH,
        )
    neighbours = jnp.where(has_left, 1, 0) + jnp.where(has_right, 1, 0)
    pl.semaphore_wait(barrier, neighbours + (ways - 1))

    def hop(way, hops, chunk, slab, own=False):
        target = {"dp": place + (1 if way == 0 else -1)}
        if chunk == chunks:
            return pltpu.make_async_remote_copy(
                src_ref=in_ref if own else in_buf.at[slab], dst_ref=in_buf.at[slab],
                send_sem=in_send.at[way, hops], recv_sem=in_recv.at[way, hops],
                device_id=target, device_id_type=pl.DeviceIdType.MESH,
            )
        band = pl.ds(chunk * CHUNK_ROWS, CHUNK_ROWS)
        return pltpu.make_async_remote_copy(
            src_ref=out_factor_ref.at[band, :] if own else of_buf.at[slab, band, :], dst_ref=of_buf.at[slab, band, :],
            send_sem=of_send.at[way, hops, chunk], recv_sem=of_recv.at[way, hops, chunk],
            device_id=target, device_id_type=pl.DeviceIdType.MESH,
        )

    for chunk in range(chunks + 1):
        @pl.when(has_right)
        def _():
            hop(0, 0, chunk, place, own=True).start()

        @pl.when(has_left)
        def _():
            hop(1, 0, chunk, place, own=True).start()

    for copy in local:
        copy.start()

    def to_peer(slab, step):
        peer = lax.rem(tensor_place + step, ways)
        return pltpu.make_async_remote_copy(
            src_ref=proj.at[slab, pl.ds(pl.multiple_of(peer * share, 8), share), :],
            dst_ref=landed.at[slab, step - 1],
            send_sem=sum_send.at[slab, step - 1], recv_sem=sum_recv.at[slab, step - 1],
            device_id={"tensor": peer}, device_id_type=pl.DeviceIdType.MESH,
        )

    def project(slab):
        tokens = g_buf.shape[0]

        def tile(index, total):
            columns = pl.ds(pl.multiple_of(index * K_TILE, LANES), K_TILE)
            return total + contract(g_buf[:, columns], of_buf[slab, :, columns])

        grad = lax.fori_loop(0, hidden // K_TILE, tile, jnp.zeros((tokens, factor_rows), jnp.float32))
        proj[slab, :, 0:factor_rows] = contract(x_buf[...], in_buf[slab])
        proj[slab, :, factor_rows:2 * factor_rows] = grad
        for step in range(1, ways):
            to_peer(slab, step).start()

    for copy in local:
        copy.wait()
    project(place)

    lane = lax.broadcasted_iota(jnp.int32, (1, LANES), 1)

    def pick(ids, base, into):
        def body(index, carry):
            number = ids[base + index]
            row = table_buf[pl.ds(lax.shift_right_logical(number, 7), 1), :]
            into[pl.ds(index, 1), :] = jnp.where(lane == jnp.bitwise_and(number, LANES - 1), row, 0.0)
            return carry
        return body

    lax.fori_loop(0, share, pick(ids_ref, tensor_place * share, tok_buf), 0)
    lax.fori_loop(0, queries, pick(query_ids_ref, 0, query_buf), 0)

    def arrive(step, carry):
        from_left = place - 1 - step
        from_right = place + 1 + step
        for chunk in range(chunks + 1):
            @pl.when(from_left >= 0)
            def _():
                hop(0, step, chunk, from_left).wait_recv()

                @pl.when(has_right)
                def _():
                    hop(0, step + 1, chunk, from_left).start()

            @pl.when(from_right < n)
            def _():
                hop(1, step, chunk, from_right).wait_recv()

                @pl.when(has_left)
                def _():
                    hop(1, step + 1, chunk, from_right).start()

        @pl.when(from_left >= 0)
        def _():
            project(from_left)

        @pl.when(from_right < n)
        def _():
            project(from_right)

        return carry

    lax.fori_loop(0, n - 1, arrive, 0)

    tok_weight = jnp.sum(tok_buf[...], axis=1, keepdims=True)
    query_weight = jnp.sum(query_buf[...], axis=1, keepdims=True)
    which = lax.broadcasted_iota(jnp.int32, (queries, LANES), 0)
    where = lax.broadcasted_iota(jnp.int32, (queries, LANES), 1)

    def finish(slab, scores):
        total = proj[slab, pl.ds(pl.multiple_of(tensor_place * share, 8), share), :]
        for step in range(1, ways):
            to_peer(slab, step).wait_recv()
            total = total + landed[slab, step - 1]
        product = total * pltpu.roll(total, factor_rows, 1)
        first = which * rank_count - slab * factor_rows
        chosen = (where >= first) & (where < first + rank_count) & (where < factor_rows)
        return scores + lax.dot_general(
            jnp.where(chosen, 1.0, 0.0), product * tok_weight, (((1,), (1,)), ((), ())),
            precision=lax.Precision.HIGHEST, preferred_element_type=jnp.float32,
        )

    scores = lax.fori_loop(0, n, finish, jnp.zeros((queries, share), jnp.float32))
    scores_ref[...] = scores * query_weight

    def drain(step, carry):
        for chunk in range(chunks + 1):
            @pl.when(has_right & (step <= place))
            def _():
                hop(0, step, chunk, place - step).wait_send()

            @pl.when(has_left & (place + step < n))
            def _():
                hop(1, step, chunk, place + step).wait_send()
        for offset in range(1, ways):
            to_peer(step, offset).wait_send()
        return carry

    lax.fori_loop(0, n, drain, 0)


def solution(mesh):
    n, ways = mesh.shape["dp"], mesh.shape["tensor"]

    def shards(train_rows, out_grads, input_factor, output_factor, train_ids, query_ids, loss_weights):
        tokens, hidden = out_grads.shape
        factor_rows, width = input_factor.shape
        queries = query_ids.shape[0]
        share = tokens // ways
        chunks = factor_rows // CHUNK_ROWS
        rank_count = factor_rows * n // queries
        table = loss_weights.reshape(-1, LANES)
        anywhere = pl.BlockSpec(memory_space=pl.ANY)
        scalars = pl.BlockSpec(memory_space=pltpu.SMEM)
        dma = pltpu.SemaphoreType.DMA
        return pl.pallas_call(
            functools.partial(kernel, n, ways, rank_count),
            out_shape=jax.ShapeDtypeStruct((queries, share), jnp.float32),
            in_specs=[anywhere] * 5 + [scalars] * 2,
            out_specs=pl.BlockSpec(memory_space=pltpu.VMEM),
            scratch_shapes=[
                pltpu.VMEM((tokens, width), jnp.bfloat16),
                pltpu.VMEM((tokens, hidden), jnp.bfloat16),
                pltpu.VMEM((n, factor_rows, width), jnp.bfloat16),
                pltpu.VMEM((n, factor_rows, hidden), jnp.bfloat16),
                pltpu.VMEM(table.shape, jnp.float32),
                pltpu.VMEM((n, tokens, 2 * factor_rows), jnp.float32),
                pltpu.VMEM((n, ways - 1, share, 2 * factor_rows), jnp.float32),
                pltpu.VMEM((share, LANES), jnp.float32),
                pltpu.VMEM((queries, LANES), jnp.float32),
                dma((5,)),
                dma((2, n)), dma((2, n)),
                dma((2, n, chunks)), dma((2, n, chunks)),
                dma((n, ways - 1)), dma((n, ways - 1)),
            ],
            compiler_params=pltpu.CompilerParams(
                collective_id=0, has_side_effects=True, vmem_limit_bytes=56 * 2**20
            ),
        )(train_rows, out_grads, input_factor, output_factor, table, train_ids, query_ids)

    return jax.shard_map(
        shards,
        mesh=mesh,
        in_specs=(
            P(("groups", "dp"), None),
            P(("groups", "dp"), "tensor"),
            P(("groups", "dp"), "tensor"),
            P(("groups", "dp"), "tensor"),
            P(("groups", "dp")),
            P("groups"),
            P(),
        ),
        out_specs=P(None, ("groups", "dp", "tensor")),
        check_vma=False,
    )
```

time: 133 us -> 82.7 us (0.62)
  Pallas kernels: 0 us -> 81.2 us
  waiting for transfers between devices: 81 us -> 0 us
  blocking collectives: 22.8 us -> 0 us
  between operations: 13.4 us -> 0.01 us
  matrix products: 5.99 us -> 0 us
  other arithmetic: 4.14 us -> 0 us
  local copies, waits for them, and re-layouts: 5.01 us -> 1.28 us
    pallas_call x0 -> x1, Pallas kernels: none -> 81.2 us  [shards(): pl.pallas_call(functools.partial(kernel, n, ways, rank_count), out_shape=...]
    all_gather x1 -> x0, waiting for transfers between devices: 50.9 us -> none  [shards(): lax.all_gather(output_factor, 'dp', axis=0, tiled=True)]
    psum x1 -> x0, waiting for transfers between devices: 29.4 us -> none  [shards(): input_whole, grad_whole = lax.psum((input_part, grad_part), 'tensor')]
    all_gather x1 -> x0, blocking collectives: 22.8 us -> none  [shards(): lax.all_gather(input_factor, 'dp', axis=0, tiled=True)]
    dot_general x2 -> x0, matrix products: 5.99 us -> none  [contract(): lax.dot_general(operand_left, operand_right, (((1,), (1,)), ((), ())), pr...]
    gather x2 -> x0, local copies, waits for them, and re-layouts: 3.41 us -> none  [the longest x1 1.77 us: shards(): tok_weight = loss_weights[own_ids]]
    mul x2 -> x0, other arithmetic: 2.17 us -> none  [the longest x1 1.51 us: shards(): input_proj * grad_proj]
    mul x1 -> x0, local copies, waits for them, and re-layouts: 1.59 us -> none  [shards(): input_proj * grad_proj]
  transfers between devices with their start and end apart: 2 -> 0, of which waited for: 2 -> 0; matrix products, arithmetic and copies ran while one was open for 5% -> 0% of each run, Pallas kernels for 0% -> 0%
where the time goes in v1:
time: 82.7 us; the launch traced here: 82.5 us
  Pallas kernels  81.2 us (98%)
  local copies, waits for them, and re-layouts  1.28 us (2%)
    pallas_call x1, Pallas kernels, shards(): pl.pallas_call(functools.partial(kernel, n, ways, rank_count), out_shape=...  81.2 us

profile of v1, /device:TPU:0, one launch (start us, length us, event | category | flops | bytes accessed | tf_op | source)
XLA Modules:
  0.0 82.5 jit_solution(11342124733668377843)
XLA Ops:
  0.0 81.2 %shard_map.73 = f32[8,64]{1,0:T(8,128)} custom-call(bf16[256,5120]{1,0:T(8,128)(2,1)} %rows_ref.1, bf16[256,6912]{1,0:T(8,128)(2,1)} %grads_ref.1, bf16[64,1280]{1,0:T(8,128)(2,1)} %in_ref.1, bf16[64,6912]{1,0:T(8,128)(2,1)} %out_factor_ref.1, f32[784,128]{1,0:T(8,128)} %bitcast.1, s32[256]{0:T(256)} %ids_ref.1, s32[8]{0:T(128)} %query_ids_ref.1), custom_call_target="tpu_custom_call" | custom-call | tf_op jit(solution)/shard_map/pallas_call | solution.py:213
  81.2 1.3 %copy.9 = f32[8,64]{1,0:T(8,128)} copy(f32[8,64]{1,0:T(8,128)} %shard_map.73) | data formatting | bytes 4096

commit v2 on v1

v2 whole, which is shorter than its diff:
```python
import functools

import jax
import jax.numpy as jnp
from jax import lax
from jax.experimental import pallas as pl
from jax.experimental.pallas import tpu as pltpu
from jax.sharding import PartitionSpec as P

LANES = 128
MOVED_PART = 3 / 8
MOVED_CHUNKS = 2
KEPT_CHUNKS = 4


def contract(left, right):
    return lax.dot_general(left, right, (((1,), (1,)), ((), ())), preferred_element_type=jnp.float32)


def column_chunks(hidden, moved):
    def cut(low, high, parts):
        tiles = (high - low) // LANES
        marks = [low + (tiles * part // parts) * LANES for part in range(parts)] + [high]
        return [(begin, end - begin) for begin, end in zip(marks[:-1], marks[1:])]

    first = cut(hidden - moved, hidden, MOVED_CHUNKS) if moved else []
    return first, cut(0, hidden - moved, KEPT_CHUNKS)


def kernel(
    n, ways, rank_count, moved,
    rows_ref, grads_ref, in_ref, out_factor_ref, table_ref, ids_ref, query_ids_ref,
    scores_ref,
    x_buf, g_buf, in_buf, of_buf, table_buf, acc, proj, landed, tok_buf, query_buf,
    guest, guest_proj, extra,
    local_sem, in_send, in_recv, of_send, of_recv, sum_send, sum_recv,
    guest_send, guest_recv, extra_send, extra_recv,
):
    place = lax.axis_index("dp")
    tensor_place = lax.axis_index("tensor")
    factor_rows, width = in_ref.shape
    hidden = out_factor_ref.shape[1]
    queries = query_ids_ref.shape[0]
    share = scores_ref.shape[1]
    kept = hidden - moved
    moved_chunks, kept_chunks = column_chunks(hidden, moved)
    chunks = moved_chunks + [None] + kept_chunks
    has_left = place > 0
    has_right = place < n - 1
    at_end = (place == 0) | (place == n - 1)
    hosting = (place == 1) | (place == n - 2)
    guest_place = jnp.where(place == 1, 0, n - 1)
    host_place = jnp.where(place == 0, 1, n - 2)
    mesh_ids = pl.DeviceIdType.MESH

    local = [
        pltpu.make_async_copy(grads_ref, g_buf, local_sem.at[0]),
        pltpu.make_async_copy(
            rows_ref.at[:, pl.ds(pl.multiple_of(tensor_place * width, LANES), width)], x_buf, local_sem.at[1]
        ),
        pltpu.make_async_copy(out_factor_ref, of_buf.at[place], local_sem.at[2]),
        pltpu.make_async_copy(in_ref, in_buf.at[place], local_sem.at[3]),
        pltpu.make_async_copy(table_ref, table_buf, local_sem.at[4]),
    ]

    barrier = pltpu.get_barrier_semaphore()

    @pl.when(has_left)
    def _():
        pl.semaphore_signal(barrier, inc=1, device_id={"dp": place - 1}, device_id_type=mesh_ids)

    @pl.when(has_right)
    def _():
        pl.semaphore_signal(barrier, inc=1, device_id={"dp": place + 1}, device_id_type=mesh_ids)

    for step in range(1, ways):
        peer = lax.rem(tensor_place + step, ways)
        pl.semaphore_signal(barrier, inc=1, device_id={"tensor": peer}, device_id_type=mesh_ids)
        if moved:
            @pl.when(at_end)
            def _():
                pl.semaphore_signal(
                    barrier, inc=1, device_id={"dp": host_place, "tensor": peer}, device_id_type=mesh_ids
                )
    greeters = jnp.where(has_left, 1, 0) + jnp.where(has_right, 1, 0) + (ways - 1)
    if moved:
        greeters = greeters + jnp.where(hosting, ways - 1, 0)
    pl.semaphore_wait(barrier, greeters)

    def hop(way, hops, chunk, slab, own=False):
        target = {"dp": place + (1 if way == 0 else -1)}
        if chunks[chunk] is None:
            return pltpu.make_async_remote_copy(
                src_ref=in_ref if own else in_buf.at[slab], dst_ref=in_buf.at[slab],
                send_sem=in_send.at[way, hops], recv_sem=in_recv.at[way, hops],
                device_id=target, device_id_type=mesh_ids,
            )
        begin, size = chunks[chunk]
        columns = pl.ds(begin, size)
        return pltpu.make_async_remote_copy(
            src_ref=out_factor_ref.at[:, columns] if own else of_buf.at[slab, :, columns],
            dst_ref=of_buf.at[slab, :, columns],
            send_sem=of_send.at[way, hops, chunk], recv_sem=of_recv.at[way, hops, chunk],
            device_id=target, device_id_type=mesh_ids,
        )

    def sends(way, chunk):
        if chunk < len(moved_chunks):
            return place < n - 2 if way == 0 else place > 1
        return has_right if way == 0 else has_left

    def takes(way, chunk, slab):
        valid = slab >= 0 if way == 0 else slab < n
        if chunk < len(moved_chunks):
            return valid & jnp.logical_not(at_end)
        return valid

    def lend(band):
        rows = pl.ds(band * share, share)
        return pltpu.make_async_remote_copy(
            src_ref=grads_ref.at[rows, pl.ds(kept, moved)], dst_ref=guest.at[rows, :],
            send_sem=guest_send.at[band], recv_sem=guest_recv.at[band],
            device_id={"dp": host_place}, device_id_type=mesh_ids,
        )

    def hand_back(band, source):
        return pltpu.make_async_remote_copy(
            src_ref=guest_proj.at[band], dst_ref=extra.at[source],
            send_sem=extra_send.at[band], recv_sem=extra_recv.at[source],
            device_id={"dp": guest_place, "tensor": band}, device_id_type=mesh_ids,
        )

    for chunk in range(len(chunks)):
        for way in range(2):
            @pl.when(sends(way, chunk))
            def _():
                hop(way, 0, chunk, place, own=True).start()

    if moved:
        @pl.when(at_end)
        def _():
            for band in range(ways):
                lend(band).start()

    for copy in local:
        copy.start()

    def to_peer(slab, step):
        peer = lax.rem(tensor_place + step, ways)
        return pltpu.make_async_remote_copy(
            src_ref=proj.at[slab, pl.ds(pl.multiple_of(peer * share, 8), share), :],
            dst_ref=landed.at[slab, step - 1],
            send_sem=sum_send.at[slab, step - 1], recv_sem=sum_recv.at[slab, step - 1],
            device_id={"tensor": peer}, device_id_type=mesh_ids,
        )

    def add_chunk(way, chunk, slab):
        if chunks[chunk] is None:
            proj[slab, :, 0:factor_rows] = contract(x_buf[...], in_buf[slab])
        else:
            begin, size = chunks[chunk]
            acc[way] += contract(g_buf[:, begin:begin + size], of_buf[slab, :, begin:begin + size])

    def send_sums(way, slab):
        proj[slab, :, factor_rows:2 * factor_rows] = acc[way]
        for step in range(1, ways):
            to_peer(slab, step).start()

    acc[...] = jnp.zeros_like(acc)
    for copy in local:
        copy.wait()
    for chunk in range(len(chunks)):
        if chunk < len(moved_chunks):
            @pl.when(jnp.logical_not(at_end))
            def _():
                add_chunk(0, chunk, place)
        else:
            add_chunk(0, chunk, place)
    send_sums(0, place)

    lane = lax.broadcasted_iota(jnp.int32, (1, LANES), 1)

    def pick(ids, base, into):
        def body(index, carry):
            number = ids[base + index]
            row = table_buf[pl.ds(lax.shift_right_logical(number, 7), 1), :]
            into[pl.ds(index, 1), :] = jnp.where(lane == jnp.bitwise_and(number, LANES - 1), row, 0.0)
            return carry
        return body

    lax.fori_loop(0, share, pick(ids_ref, tensor_place * share, tok_buf), 0)
    lax.fori_loop(0, queries, pick(query_ids_ref, 0, query_buf), 0)

    def arrive(step, carry):
        slabs = (place - 1 - step, place + 1 + step)
        acc[...] = jnp.zeros_like(acc)
        for chunk in range(len(chunks)):
            for way in range(2):
                @pl.when(takes(way, chunk, slabs[way]))
                def _():
                    hop(way, step, chunk, slabs[way]).wait_recv()

                    @pl.when(sends(way, chunk))
                    def _():
                        hop(way, step + 1, chunk, slabs[way]).start()

                    add_chunk(way, chunk, slabs[way])
                    if chunk == len(chunks) - 1:
                        send_sums(way, slabs[way])
        return carry

    lax.fori_loop(0, n - 1, arrive, 0)

    if moved:
        @pl.when(hosting)
        def _():
            for band in range(ways):
                lend(band).wait_recv()
                tokens = guest[band * share:(band + 1) * share, :]

                def pair(index, carry):
                    factors = of_buf[pl.ds(index * 2, 2), :, kept:hidden].reshape(2 * factor_rows, moved)
                    guest_proj[band, index] = contract(tokens, factors)
                    return carry

                lax.fori_loop(0, n // 2, pair, 0)
                hand_back(band, tensor_place).start()

    tok_weight = jnp.sum(tok_buf[...], axis=1, keepdims=True)
    query_weight = jnp.sum(query_buf[...], axis=1, keepdims=True)
    which = lax.broadcasted_iota(jnp.int32, (queries, LANES), 0)
    where = lax.broadcasted_iota(jnp.int32, (queries, LANES), 1)

    def finish(slab, scores):
        total = proj[slab, pl.ds(pl.multiple_of(tensor_place * share, 8), share), :]
        for step in range(1, ways):
            to_peer(slab, step).wait_recv()
            total = total + landed[slab, step - 1]
        proj[slab, pl.ds(pl.multiple_of(tensor_place * share, 8), share), :] = total
        return scores

    lax.fori_loop(0, n, finish, 0)

    if moved:
        @pl.when(at_end)
        def _():
            for source in range(ways):
                hand_back(tensor_place, source).wait_recv()

            def add_extra(slab, carry):
                pair = lax.div(slab, 2)
                more = extra[0, pair]
                for source in range(1, ways):
                    more = more + extra[source, pair]
                more = jnp.where(lax.rem(slab, 2) == 0, pltpu.roll(more, factor_rows, 1), more)
                rows = pl.ds(pl.multiple_of(tensor_place * share, 8), share)
                proj[slab, rows, :] += jnp.where(lane >= factor_rows, more, 0.0)
                return carry

            lax.fori_loop(0, n, add_extra, 0)

    def score(slab, scores):
        total = proj[slab, pl.ds(pl.multiple_of(tensor_place * share, 8), share), :]
        product = total * pltpu.roll(total, factor_rows, 1)
        first = which * rank_count - slab * factor_rows
        chosen = (where >= first) & (where < first + rank_count) & (where < factor_rows)
        chosen = chosen & (first >= 0)
        return scores + lax.dot_general(
            jnp.where(chosen, 1.0, 0.0), product * tok_weight, (((1,), (1,)), ((), ())),
            precision=lax.Precision.HIGHEST, preferred_element_type=jnp.float32,
        )

    scores = lax.fori_loop(0, n, score, jnp.zeros((queries, share), jnp.float32))
    scores_ref[...] = scores * query_weight

    def drain(step, carry):
        for chunk in range(len(chunks)):
            for way in range(2):
                slab = place - step if way == 0 else place + step
                @pl.when(sends(way, chunk) & ((slab >= 0) & (slab < n)))
                def _():
                    hop(way, step, chunk, slab).wait_send()
        for offset in range(1, ways):
            to_peer(step, offset).wait_send()
        return carry

    lax.fori_loop(0, n, drain, 0)

    if moved:
        @pl.when(at_end)
        def _():
            for band in range(ways):
                lend(band).wait_send()

        @pl.when(hosting)
        def _():
            for band in range(ways):
                hand_back(band, tensor_place).wait_send()


def solution(mesh):
    n, ways = mesh.shape["dp"], mesh.shape["tensor"]

    def shards(train_rows, out_grads, input_factor, output_factor, train_ids, query_ids, loss_weights):
        tokens, hidden = out_grads.shape
        factor_rows, width = input_factor.shape
        queries = query_ids.shape[0]
        share = tokens // ways
        moved = int(hidden // LANES * MOVED_PART) * LANES if n >= 4 and n % 2 == 0 else 0
        count = sum(len(part) for part in column_chunks(hidden, moved)) + 1
        rank_count = factor_rows * n // queries
        table = loss_weights.reshape(-1, LANES)
        anywhere = pl.BlockSpec(memory_space=pl.ANY)
        scalars = pl.BlockSpec(memory_space=pltpu.SMEM)
        dma = pltpu.SemaphoreType.DMA
        pairs = (ways, max(n // 2, 1), share, 2 * factor_rows)
        return pl.pallas_call(
            functools.partial(kernel, n, ways, rank_count, moved),
            out_shape=jax.ShapeDtypeStruct((queries, share), jnp.float32),
            in_specs=[anywhere] * 5 + [scalars] * 2,
            out_specs=pl.BlockSpec(memory_space=pltpu.VMEM),
            scratch_shapes=[
                pltpu.VMEM((tokens, width), jnp.bfloat16),
                pltpu.VMEM((tokens, hidden), jnp.bfloat16),
                pltpu.VMEM((n, factor_rows, width), jnp.bfloat16),
                pltpu.VMEM((n, factor_rows, hidden), jnp.bfloat16),
                pltpu.VMEM(table.shape, jnp.float32),
                pltpu.VMEM((2, tokens, factor_rows), jnp.float32),
                pltpu.VMEM((n, tokens, 2 * factor_rows), jnp.float32),
                pltpu.VMEM((n, ways - 1, share, 2 * factor_rows), jnp.float32),
                pltpu.VMEM((share, LANES), jnp.float32),
                pltpu.VMEM((queries, LANES), jnp.float32),
                pltpu.VMEM((tokens, max(moved, LANES)), jnp.bfloat16),
                pltpu.VMEM(pairs, jnp.float32),
                pltpu.VMEM(pairs, jnp.float32),
                dma((5,)),
                dma((2, n)), dma((2, n)),
                dma((2, n, count)), dma((2, n, count)),
                dma((n, ways - 1)), dma((n, ways - 1)),
                dma((ways,)), dma((ways,)), dma((ways,)), dma((ways,)),
            ],
            compiler_params=pltpu.CompilerParams(
                collective_id=0, has_side_effects=True, vmem_limit_bytes=58 * 2**20
            ),
        )(train_rows, out_grads, input_factor, output_factor, table, train_ids, query_ids)

    return jax.shard_map(
        shards,
        mesh=mesh,
        in_specs=(
            P(("groups", "dp"), None),
            P(("groups", "dp"), "tensor"),
            P(("groups", "dp"), "tensor"),
            P(("groups", "dp"), "tensor"),
            P(("groups", "dp")),
            P("groups"),
            P(),
        ),
        out_specs=P(None, ("groups", "dp", "tensor")),
        check_vma=False,
    )
```

time: 82.7 us -> 67.7 us (0.82)
  Pallas kernels: 81.2 us -> 65.4 us
    pallas_call x1, Pallas kernels: 81.2 us -> 65.4 us  [shards(): pl.pallas_call(functools.partial(kernel, n, ways, rank_count, moved), out...]
where the time goes in v2:
time: 67.7 us; the launch traced here: 66.7 us
  Pallas kernels  65.4 us (97%)
  local copies, waits for them, and re-layouts  1.28 us (2%)
    pallas_call x1, Pallas kernels, shards(): pl.pallas_call(functools.partial(kernel, n, ways, rank_count, moved), out...  65.4 us

profile of v2, /device:TPU:0, one launch (start us, length us, event | category | flops | bytes accessed | tf_op | source)
XLA Modules:
  0.0 66.7 jit_solution(17600259829754706990)
XLA Ops:
  0.0 65.4 %shard_map.73 = f32[8,64]{1,0:T(8,128)} custom-call(bf16[256,5120]{1,0:T(8,128)(2,1)} %rows_ref.1, bf16[256,6912]{1,0:T(8,128)(2,1)} %grads_ref.1, bf16[64,1280]{1,0:T(8,128)(2,1)} %in_ref.1, bf16[64,6912]{1,0:T(8,128)(2,1)} %out_factor_ref.1, f32[784,128]{1,0:T(8,128)} %bitcast.1, s32[256]{0:T(256)} %ids_ref.1, s32[8]{0:T(128)} %query_ids_ref.1), custom_call_target="tpu_custom_call" | custom-call | tf_op jit(solution)/shard_map/pallas_call | solution.py:317
  65.4 1.3 %copy.9 = f32[8,64]{1,0:T(8,128)} copy(f32[8,64]{1,0:T(8,128)} %shard_map.73) | data formatting | bytes 4096

commit v3 on v2

--- a/solution.py
+++ b/solution.py
@@ -8,7 +8,7 @@
 from jax.sharding import PartitionSpec as P
 
 LANES = 128
-MOVED_PART = 3 / 8
+MOVED_PART = 5 / 16
 MOVED_CHUNKS = 2
 KEPT_CHUNKS = 4
 
@@ -30,7 +30,7 @@
 def kernel(
     n, ways, rank_count, moved,
     rows_ref, grads_ref, in_ref, out_factor_ref, table_ref, ids_ref, query_ids_ref,
-    scores_ref,
+    scores_ref, query_weight_ref,
     x_buf, g_buf, in_buf, of_buf, table_buf, acc, proj, landed, tok_buf, query_buf,
     guest, guest_proj, extra,
     local_sem, in_send, in_recv, of_send, of_recv, sum_send, sum_recv,
@@ -271,7 +271,8 @@
         )
 
     scores = lax.fori_loop(0, n, score, jnp.zeros((queries, share), jnp.float32))
-    scores_ref[...] = scores * query_weight
+    scores_ref[...] = scores
+    query_weight_ref[...] = jnp.broadcast_to(query_weight, scores.shape)
 
     def drain(step, carry):
         for chunk in range(len(chunks)):
@@ -314,11 +315,11 @@
         scalars = pl.BlockSpec(memory_space=pltpu.SMEM)
         dma = pltpu.SemaphoreType.DMA
         pairs = (ways, max(n // 2, 1), share, 2 * factor_rows)
-        return pl.pallas_call(
+        scores, query_weight = pl.pallas_call(
             functools.partial(kernel, n, ways, rank_count, moved),
-            out_shape=jax.ShapeDtypeStruct((queries, share), jnp.float32),
+            out_shape=[jax.ShapeDtypeStruct((queries, share), jnp.float32)] * 2,
             in_specs=[anywhere] * 5 + [scalars] * 2,
-            out_specs=pl.BlockSpec(memory_space=pltpu.VMEM),
+            out_specs=[pl.BlockSpec(memory_space=pltpu.VMEM)] * 2,
             scratch_shapes=[
                 pltpu.VMEM((tokens, width), jnp.bfloat16),
                 pltpu.VMEM((tokens, hidden), jnp.bfloat16),
@@ -343,6 +344,7 @@
                 collective_id=0, has_side_effects=True, vmem_limit_bytes=58 * 2**20
             ),
         )(train_rows, out_grads, input_factor, output_factor, table, train_ids, query_ids)
+        return scores * query_weight
 
     return jax.shard_map(
         shards,

time: 67.7 us -> 67.8 us (level)
  other arithmetic: 0 us -> 1.29 us
  local copies, waits for them, and re-layouts: 1.28 us -> 0 us
    mul x0 -> x1, other arithmetic: none -> 1.29 us  [shards(): return scores * query_weight]
    unnamed x1 -> x0, local copies, waits for them, and re-layouts: 1.28 us -> none
where the time goes in v3:
time: 67.8 us; the launch traced here: 67 us
  Pallas kernels  65.6 us (97%)
  other arithmetic  1.29 us (2%)
    pallas_call x1, Pallas kernels, shards(): pl.pallas_call(functools.partial(kernel, n, ways, rank_count, moved), out...  65.6 us

profile of v3, /device:TPU:0, one launch (start us, length us, event | category | flops | bytes accessed | tf_op | source)
XLA Modules:
  0.0 67.0 jit_solution(5918641826457461085)
XLA Ops:
  0.0 65.6 %shard_map.73 = (f32[8,64]{1,0:T(8,128)}, f32[8,64]{1,0:T(8,128)}) custom-call(bf16[256,5120]{1,0:T(8,128)(2,1)} %rows_ref.1, bf16[256,6912]{1,0:T(8,128)(2,1)} %grads_ref.1, bf16[64,1280]{1,0:T(8,128)(2,1)} %in_ref.1, bf16[64,6912]{1,0:T(8,128)(2,1)} %out_factor_ref.1, f32[784,128]{1,0:T(8,128)} %bitcast.1, s32[256]{0:T(256)} %ids_ref.1, s32[8]{0:T(128)} %query_ids_ref.1), custom_call_target="tpu_custom_call" | custom-call | tf_op jit(solution)/shard_map/pallas_call | solution.py:318
  65.7 1.3 %mul.3 = f32[8,64]{1,0:T(8,128)} multiply(f32[8,64]{1,0:T(8,128)} %get-tuple-element.7, f32[8,64]{1,0:T(8,128)} %get-tuple-element.8) | non-fusion elementwise | flops 512 | bytes 6144 | tf_op jit(solution)/shard_map/mul | solution.py:347
